TPU v7x, 512 devices: a whole 4x8x8 slice. The times are simulated.
512 devices in a mesh: rec: 16 (over z, core), frame: 32 (over x, y).
Axes of the slice: x: 4, y: 8, z: 8, core: 2. Of those that a mesh axis runs over, the one named last changes fastest.
Arguments:
- frames: bfloat16 [16, 49152, 256], P('rec', 'frame'), may hold values from -10 to 10
- texts: bfloat16 [32, 224, 256], P('rec', 'frame'), may hold values from -100 to 100
- pair_rec: int32 [32, 1], replicated, may hold values from 0 to 15, as said below
- pair_text: int32 [32], replicated, may hold values from 0 to 31, as said below
- pair_label: int32 [32], replicated, may hold values 0 or 1
Outputs:
- loss: float32 [], replicated
- grad_frames: bfloat16 [16, 49152, 256], P('rec', 'frame')
- grad_texts: bfloat16 [32, 224, 256], P('rec', 'frame')
Inputs may be any that keep to these rules, and one draw needn't show every extreme that they name: `pair_rec`: no recording is named by more than 6 pairs, some recording by exactly 6, and every recording by at least one. A pair's text is held by the index of rec one after, one before, or 8 after its recording (counted round): pair_text // 2 = (pair_rec + k) mod 16 with k one of 1, 15, 8.
All inputs are finite; a program needn't handle non-finite values.
Results may differ from a plain program's by a relative error of at most 0.0085.
Values may be sent and summed in bfloat16 or wider, within the bound.
A program may use at most 64 MiB of HBM per device.

v0:
```python
import jax
import jax.numpy as jnp
from jax import lax
from jax.sharding import PartitionSpec as P

MOST = 6
EPS = 1e-06
TEMP = 10.0
BIAS = -1.0
LOSS_SCALE = 2048.0


def slot_tables(pair_rec, pair_text, pair_label, here, most):
    record = pair_rec[:, 0]
    count = record.shape[0]
    order = jnp.arange(count, dtype=jnp.int32)
    same = (record[:, None] == record[None, :]).astype(jnp.int32)
    earlier = (order[None, :] < order[:, None]).astype(jnp.int32)
    rank = jnp.sum(same * earlier, axis=1)
    places = jnp.arange(most, dtype=jnp.int32)
    chosen = ((record[None, :] == here) & (rank[None, :] == places[:, None])).astype(jnp.int32)
    valid = jnp.sum(chosen, axis=1)
    slot_text = jnp.sum(chosen * pair_text[None, :], axis=1)
    sign = jnp.sum(chosen * (2 * pair_label[None, :] - 1), axis=1)
    return (valid, slot_text, sign)


def pair_terms(score, valid, sign, tokens):
    margin = -sign * (TEMP * score + BIAS)
    loss_part = valid * jax.nn.softplus(margin)
    grad_cos = -LOSS_SCALE * TEMP * valid * sign * jax.nn.sigmoid(margin) / tokens
    return (loss_part, grad_cos)


def body(frames, texts, pair_rec, pair_text, pair_label):
    here = lax.axis_index("rec")
    part = lax.axis_index("frame")
    owned, width_rows, width = texts.shape
    tokens = width_rows * lax.axis_size("frame")
    n_text = owned * lax.axis_size("rec")
    valid, slot_text, sign = slot_tables(pair_rec, pair_text, pair_label, here, MOST)
    valid_f = valid.astype(jnp.float32)
    sign_f = sign.astype(jnp.float32)
    picks = (
        (slot_text[:, None] == jnp.arange(n_text, dtype=jnp.int32)[None, :]) & (valid[:, None] > 0)
    ).astype(jnp.bfloat16)
    whole = lax.all_gather(texts, "frame", axis=1, tiled=True)
    query_vectors = jnp.einsum(
        "jc,cgx->jgx",
        picks,
        lax.all_gather(whole, "rec", axis=0, tiled=True),
        preferred_element_type=jnp.float32,
    ).astype(jnp.bfloat16)
    upstream_signal = frames[0]
    logit_scale = width ** (-0.5)
    pair_scores = (
        jnp.einsum(
            "ype,je->ypj", query_vectors, upstream_signal, preferred_element_type=jnp.float32
        )
        * logit_scale
    )
    local_max = jnp.max(pair_scores, axis=2)
    row_max = lax.pmax(local_max, "frame")
    expo = jnp.exp(pair_scores - row_max[..., None])
    batch_weights = expo.astype(jnp.bfloat16)
    value_partial = jnp.einsum(
        "pqx,xh->pqh", batch_weights, upstream_signal, preferred_element_type=jnp.float32
    )
    query_f = query_vectors.astype(jnp.float32)
    q_norm = lax.rsqrt(jnp.sum(query_f * query_f, axis=2) + EPS)
    q_unit = query_f * q_norm[..., None]
    context = lax.psum(value_partial, "frame")
    c_norm = lax.rsqrt(jnp.sum(context * context, axis=2) + EPS)
    c_unit = context * c_norm[..., None]
    cos = jnp.sum(q_unit * c_unit, axis=2)
    score = jnp.mean(cos, axis=1)
    loss_part, grad_cos = pair_terms(score, valid_f, sign_f, tokens)
    weight = grad_cos[:, None, None]
    d_context = weight * (q_unit - cos[..., None] * c_unit) * c_norm[..., None]
    direct = weight * (c_unit - cos[..., None] * q_unit) * q_norm[..., None]
    direct_own = lax.dynamic_slice_in_dim(direct, part * width_rows, width_rows, 1)
    context_batch_gradient = d_context.astype(jnp.bfloat16)
    weight_gradient = jnp.einsum(
        "ype,je->ypj", context_batch_gradient, upstream_signal, preferred_element_type=jnp.float32
    )
    score_gradient = (expo * weight_gradient * logit_scale).astype(jnp.bfloat16)
    d_query = lax.psum_scatter(
        jnp.einsum(
            "slf,fd->lsd", score_gradient, upstream_signal, preferred_element_type=jnp.float32
        ),
        "frame",
        scatter_dimension=0,
        tiled=True,
    )
    d_query = d_query + jnp.transpose(direct_own, (1, 0, 2))
    text_term = jnp.einsum(
        "st,lsd->tld", picks.astype(jnp.float32), d_query, precision=lax.Precision.HIGHEST
    )
    grad_texts = lax.psum_scatter(text_term, "rec", scatter_dimension=0, tiled=True).astype(
        jnp.bfloat16
    )
    frame_loss_piece = jnp.einsum(
        "cvm,cvz->mz", score_gradient, query_vectors, preferred_element_type=jnp.float32
    )
    frame_loss_piece = frame_loss_piece + jnp.einsum(
        "cvm,cvz->mz", batch_weights, context_batch_gradient, preferred_element_type=jnp.float32
    )
    grad_frames = frame_loss_piece.astype(jnp.bfloat16)[None]
    loss = lax.psum(jnp.sum(loss_part), "rec")
    return (loss, grad_frames, grad_texts)


def solution(mesh):
    return jax.shard_map(
        body,
        mesh=mesh,
        in_specs=(P("rec", "frame", None), P("rec", "frame", None), P(), P(), P()),
        out_specs=(P(), P("rec", "frame", None), P("rec", "frame", None)),
        check_vma=False,
    )
```

profile of v0, /device:TPU:16, one launch (start us, length us, event | category | flops | bytes accessed | tf_op | source)
XLA Modules:
  0.0 644.4 jit_solution(15901261809968272552)
XLA Ops:
  7.2 0.0 copy-start
  7.2 0.0 all-gather.2.cloned.1.call-start
  7.2 49.8 %all_gather.6 = bf16[2,224,256]{2,0,1:T(2,128)(2,1)S(1)} all-gather(bf16[2,7,256]{2,0,1:T(2,128)(2,1)} %param.6), channel_id=1, replica_groups=mesh['rec'=16,'frame'=32] {'frame'}, dimensions={1}, use_global_device_ids=true | all-gather | bytes 236544 | tf_op jit(solution)/shard_map/all_gather | solution.py:47
  57.0 0.7 copy.20
  57.7 0.0 all-gather.2.cloned.1.call-update
  57.8 0.0 all-reduce.5.cloned.1.call-start
  57.8 0.9 select_reduce_fusion
  58.7 0.7 broadcast_compare_fusion.1
  59.4 0.7 multiply_add_fusion
  60.1 1.3 select_reduce_fusion.2
  61.4 0.0 copy-start.8
  61.4 43.4 %all-gather.2.cloned.1.call-done = bf16[32,224,256]{2,1,0:T(8,128)(2,1)} async-done(((bf16[2,224,256]{2,1,0:T(8,128)(2,1)}), bf16[32,224,256]{2,1,0:T(8,128)(2,1)}) %all-gather.2.cloned.1.call-update) | async-done | bytes 3670032 | tf_op jit(solution)/shard_map/all_gather | solution.py:51
  104.7 0.0 copy-done.9
  104.7 4.3 fusion.6
  109.0 0.0 copy-done.4
  109.0 0.0 copy-done.8
  109.0 0.0 copy-done
  109.0 4.4 multiply_reduce_fusion
  113.4 71.4 %pmax.7 = f32[6,224]{1,0:T(8,128)S(1)} all-reduce(f32[6,224]{1,0:T(8,128)S(1)} %get-tuple-element.17), channel_id=1, replica_groups=mesh['rec'=16,'frame'=32] {'frame'}, use_global_device_ids=true, to_apply=%region_6.0 | all-reduce | flops 1344 | bytes 10752 | tf_op jit(solution)/shard_map/pmax | solution.py:63
  184.8 4.9 fusion.13
  189.7 2.1 copy.23
  191.7 0.0 all-reduce.5.cloned.1.call-update
  191.8 0.2 reduce-scatter.3.cloned.1.call-start
  192.0 0.7 add_rsqrt_fusion.1
  192.6 157.1 %all-reduce.5.cloned.1.call-done = f32[6,224,256]{2,0,1:T(8,128)} async-done(((f32[6,224,256]{2,0,1:T(8,128)}), f32[6,224,256]{2,0,1:T(8,128)}) %all-reduce.5.cloned.1.call-update) | async-done | bytes 1376272 | tf_op jit(solution)/shard_map/psum | solution.py:72
  349.7 1.9 multiply_reduce_fusion.1
  351.6 2.4 multiply_reduce_fusion.2
  354.0 1.4 fusion.44
  355.4 0.0 copy-done.1
  355.4 1.8 convert_multiply_fusion
  357.2 4.9 multiply_convert_fusion
  362.2 1.3 fusion.10
  363.5 0.7 copy-done.10
  364.2 2.1 copy.47
  366.2 0.0 reduce-scatter.3.cloned.1.call-update
  366.2 1.3 dynamic-slice
  368.2 0.7 constant_dynamic-slice_fusion
  368.9 0.7 constant_dynamic-slice_fusion.1
  369.6 5.7 convolution_bitcast_fusion
  375.2 0.0 copy-done.11
  375.3 0.0 copy-start.5
  375.3 0.0 copy-start.7
  375.3 2.3 fusion.5
  377.6 209.2 %reduce-scatter.3.cloned.1.call-done = f32[7,6,256]{2,1,0:T(8,128)} async-done(((f32[224,6,256]{2,1,0:T(8,128)}), f32[7,6,256]{2,1,0:T(8,128)}) %reduce-scatter.3.cloned.1.call-update) | async-done | bytes 43024 | tf_op jit(solution)/shard_map/reduce_scatter | solution.py:87
  586.9 0.0 copy-done.7
  586.9 1.3 fusion.27
  588.2 49.1 %all-reduce.6 = (f32[]{:T(128)}, bf16[32,7,256]{2,0,1:T(8,128)(2,1)S(1)}) all-reduce(f32[]{:T(128)} %get-tuple-element.14, f32[32,7,256]{2,0,1:T(8,128)S(1)} %fusion.27), channel_id=1, replica_groups=mesh['rec'=16,'frame'=32] {'rec'}, use_global_device_ids=true, to_apply=%region_11.12 | all-reduce | flops 57345 | bytes 344072 | tf_op jit(solution)/shard_map/psum | solution.py:109
  637.3 0.6 dynamic-slice_convert_fusion
  (14 shorter events, 0.1 us)
Async XLA Ops:
  7.2 101.8 %copy-start = (bf16[1,1536,256]{2,1,0:T(8,128)(2,1)S(1)}, bf16[1,1536,256]{2,1,0:T(8,128)(2,1)}, u32[]{:S(2)}) copy-start(bf16[1,1536,256]{2,1,0:T(8,128)(2,1)} %param.5) | copy-start | bytes 2359300
  7.2 97.5 %all-gather.2.cloned.1.call-start = ((), (), s32[]{:S(2)}) async-start(), calls=%async_computation.1 | async-start | bytes 3899392 | tf_op jit(solution)/shard_map/all_gather | solution.py:51
  57.8 291.9 %all-reduce.5.cloned.1.call-start = ((), (), s32[]{:S(2)}) async-start(), calls=%async_computation.2 | async-start | bytes 3670016 | tf_op jit(solution)/shard_map/psum | solution.py:72
  61.3 43.4 %copy-start.9 = (s32[6]{0:T(128)}, s32[6]{0:T(128)S(1)}, u32[]{:S(2)}) copy-start(s32[6]{0:T(128)S(1)} %get-tuple-element.7) | copy-start | bytes 76
  61.3 47.6 %copy-start.4 = (s32[6]{0:T(128)}, s32[6]{0:T(128)S(1)}, u32[]{:S(2)}) copy-start(s32[6]{0:T(128)S(1)} %get-tuple-element.6) | copy-start | bytes 76
  61.4 47.6 %copy-start.8 = (pred[6]{0:T(512)(128)(4,1)}, pred[6]{0:T(512)(128)(4,1)S(1)}, u32[]{:S(2)}) copy-start(pred[6]{0:T(512)(128)(4,1)S(1)} %broadcast_compare_fusion) | copy-start | bytes 22
  191.8 395.1 %reduce-scatter.3.cloned.1.call-start = ((), (), s32[]{:S(2)}) async-start(), calls=%async_computation.3 | async-start | bytes 1892352 | tf_op jit(solution)/shard_map/reduce_scatter | solution.py:87
  349.7 5.7 copy-start.1
  354.0 3.2 copy-start.3
  355.4 6.8 %copy-start.6 = (f32[6]{0:T(128)}, f32[6]{0:T(128)S(1)}, u32[]{:S(2)}) copy-start(f32[6]{0:T(128)S(1)} %get-tuple-element.13) | copy-start | bytes 76
  357.2 5.0 copy-start.2
  362.2 2.0 copy-start.10
  369.6 5.7 copy-start.11
  375.3 211.6 %copy-start.5 = (s32[6]{0:T(128)S(1)}, s32[6]{0:T(128)}, u32[]{:S(2)}) copy-start(s32[6]{0:T(128)} %copy-done.4) | copy-start | bytes 76
  375.3 211.6 %copy-start.7 = (f32[6]{0:T(128)S(1)}, f32[6]{0:T(128)}, u32[]{:S(2)}) copy-start(f32[6]{0:T(128)} %copy-done.6) | copy-start | bytes 76
Sparse Core Ops, SparseCore 0:
  57.9 46.7 all-gather.1
  191.9 157.7 all-reduce.4
  366.4 220.4 reduce-scatter.2
where the time goes:
time: 645 us; the launch traced here: 644 us
  waiting for transfers between devices  410 us (64%)
  blocking collectives  170 us (26%)
  matrix products  29 us (4%)
  between operations  14.6 us (2%)
  other arithmetic  11.7 us (2%)
  local copies, waits for them, and re-layouts  8.88 us (1%)
    reduce_scatter x1, waiting for transfers between devices, body(): lax.psum_scatter(jnp.einsum('slf,fd->lsd', score_gradient, upstream_signa...  209 us
    psum x1, waiting for transfers between devices, body(): context = lax.psum(value_partial, 'frame')  157 us
    pmax x1, blocking collectives, body(): row_max = lax.pmax(local_max, 'frame')  71.4 us
    all_gather x1, blocking collectives, body(): whole = lax.all_gather(texts, 'frame', axis=1, tiled=True)  49.8 us
    psum x1, blocking collectives, body(): loss = lax.psum(jnp.sum(loss_part), 'rec')  49.1 us
    all_gather x1, waiting for transfers between devices, body(): lax.all_gather(whole, 'rec', axis=0, tiled=True)  43.4 us
  transfers between devices with their start and end apart: 3, of which 3 were waited for; matrix products, arithmetic and copies ran while one was open for 2% of the time, Pallas kernels for 0%

commit v1 on v0

--- a/solution.py
+++ b/solution.py
@@ -69,7 +69,7 @@
     query_f = query_vectors.astype(jnp.float32)
     q_norm = lax.rsqrt(jnp.sum(query_f * query_f, axis=2) + EPS)
     q_unit = query_f * q_norm[..., None]
-    context = lax.psum(value_partial, "frame")
+    context = jnp.sum(lax.all_gather(value_partial, "frame"), axis=0)
     c_norm = lax.rsqrt(jnp.sum(context * context, axis=2) + EPS)
     c_unit = context * c_norm[..., None]
     cos = jnp.sum(q_unit * c_unit, axis=2)

time: 645 us -> 796 us (1.23)
  waiting for transfers between devices: 410 us -> 549 us
  other arithmetic: 11.7 us -> 25.3 us
    all_gather x0 -> x1, waiting for transfers between devices: none -> 294 us  [body(): context = jnp.sum(lax.all_gather(value_partial, 'frame'), axis=0)]
    psum x1 -> x0, waiting for transfers between devices: 157 us -> none  [body(): context = lax.psum(value_partial, 'frame')]
    reduce_sum x0 -> x1, other arithmetic: none -> 16.2 us  [body(): context = jnp.sum(lax.all_gather(value_partial, 'frame'), axis=0)]
where the time goes in v1:
time: 796 us; the launch traced here: 795 us
  waiting for transfers between devices  549 us (69%)
  blocking collectives  170 us (21%)
  matrix products  30 us (4%)
  other arithmetic  25.3 us (3%)
  between operations  14.6 us (2%)
    all_gather x1, waiting for transfers between devices, body(): context = jnp.sum(lax.all_gather(value_partial, 'frame'), axis=0)  294 us
    reduce_scatter x1, waiting for transfers between devices, body(): lax.psum_scatter(jnp.einsum('slf,fd->lsd', score_gradient, upstream_signa...  211 us
    pmax x1, blocking collectives, body(): row_max = lax.pmax(local_max, 'frame')  71.4 us
    all_gather x1, blocking collectives, body(): whole = lax.all_gather(texts, 'frame', axis=1, tiled=True)  49.8 us
    psum x1, blocking collectives, body(): loss = lax.psum(jnp.sum(loss_part), 'rec')  49.1 us
    all_gather x1, waiting for transfers between devices, body(): lax.all_gather(whole, 'rec', axis=0, tiled=True)  43.8 us
    reduce_sum x1, other arithmetic, body(): context = jnp.sum(lax.all_gather(value_partial, 'frame'), axis=0)  16.2 us
  transfers between devices with their start and end apart: 3, of which 3 were waited for; matrix products, arithmetic and copies ran while one was open for 2% of the time, Pallas kernels for 0%

profile of v1, /device:TPU:16, one launch (start us, length us, event | category | flops | bytes accessed | tf_op | source)
XLA Modules:
  0.0 795.1 jit_solution(5661618880199912505)
XLA Ops:
  7.2 0.0 copy-start
  7.2 0.0 all-gather.4.cloned.1.call-start
  7.2 49.8 %all_gather.12 = bf16[2,224,256]{2,0,1:T(2,128)(2,1)S(1)} all-gather(bf16[2,7,256]{2,0,1:T(2,128)(2,1)} %param.6), channel_id=1, replica_groups=mesh['rec'=16,'frame'=32] {'frame'}, dimensions={1}, use_global_device_ids=true | all-gather | bytes 236544 | tf_op jit(solution)/shard_map/all_gather | solution.py:47
  57.0 0.7 copy.49
  57.7 0.0 all-gather.4.cloned.1.call-update
  57.8 0.0 all-gather.6.cloned.1.call-start
  57.8 0.9 select_reduce_fusion
  58.7 0.7 multiply_add_fusion
  59.4 0.7 broadcast_compare_fusion.1
  60.1 0.8 select_reduce_fusion.2
  60.9 43.8 %all-gather.4.cloned.1.call-done = bf16[32,224,256]{2,1,0:T(8,128)(2,1)} async-done(((bf16[2,224,256]{2,1,0:T(8,128)(2,1)}), bf16[32,224,256]{2,1,0:T(8,128)(2,1)}) %all-gather.4.cloned.1.call-update) | async-done | bytes 3670032 | tf_op jit(solution)/shard_map/all_gather | solution.py:51
  104.7 4.3 fusion.6
  109.0 0.0 copy-done
  109.0 4.6 multiply_reduce_fusion
  113.5 71.4 %pmax.7 = f32[6,224]{1,0:T(8,128)S(1)} all-reduce(f32[6,224]{1,0:T(8,128)S(1)} %get-tuple-element.17), channel_id=1, replica_groups=mesh['rec'=16,'frame'=32] {'frame'}, use_global_device_ids=true, to_apply=%region_6.0 | all-reduce | flops 1344 | bytes 10752 | tf_op jit(solution)/shard_map/pmax | solution.py:63
  184.9 5.9 fusion.13
  190.8 0.0 all-gather.6.cloned.1.call-update
  190.8 0.2 reduce-scatter.3.cloned.1.call-start
  191.1 0.1 copy.51
  191.2 0.1 copy.52
  191.3 293.6 %all-gather.6.cloned.1.call-done = f32[192,224,256]{2,1,0:T(8,128)} async-done(((f32[6,224,256]{2,1,0:T(8,128)}), f32[192,224,256]{2,1,0:T(8,128)}) %all-gather.6.cloned.1.call-update) | async-done | bytes 44040208 | tf_op jit(solution)/shard_map/all_gather | solution.py:72
  485.0 16.2 %reduce_sum.95 = f32[6,224,256]{2,1,0:T(8,128)S(1)} reduce(f32[32,6,224,256]{3,2,1,0:T(8,128)} %bitcast.44, f32[]{:T(128)} %constant.14.clone.1), dimensions={0}, to_apply=%region_7.0 | reduce | flops 10665984 | bytes 45416452 | tf_op jit(solution)/shard_map/reduce_sum | solution.py:72
  501.2 0.3 multiply_reduce_fusion.1
  501.5 0.1 copy.54
  501.6 2.4 multiply_reduce_fusion.2
  504.0 0.6 fusion.44
  504.6 2.7 copy_multiply_fusion
  507.3 0.0 copy-start.1
  507.3 4.9 multiply_convert_fusion
  512.3 0.0 copy-done.1
  512.3 0.0 copy-start.3
  512.3 1.3 fusion.10
  513.6 0.7 copy-done.3
  514.2 0.0 copy-start.2
  514.2 2.1 copy.86
  516.4 0.0 reduce-scatter.3.cloned.1.call-update
  516.4 1.3 dynamic-slice
  518.4 0.0 copy-done.2
  518.4 0.0 copy-start.4
  518.4 5.5 convolution_bitcast_fusion
  523.9 0.0 copy-done.4
  523.9 2.4 fusion.5
  526.2 211.3 %reduce-scatter.3.cloned.1.call-done = f32[7,6,256]{2,1,0:T(8,128)} async-done(((f32[224,6,256]{2,1,0:T(8,128)}), f32[7,6,256]{2,1,0:T(8,128)}) %reduce-scatter.3.cloned.1.call-update) | async-done | bytes 43024 | tf_op jit(solution)/shard_map/reduce_scatter | solution.py:87
  737.5 1.3 fusion.27
  738.8 49.1 %all-reduce.3 = (f32[]{:T(128)}, bf16[32,7,256]{2,0,1:T(8,128)(2,1)S(1)}) all-reduce(f32[]{:T(128)} %get-tuple-element.14, f32[32,7,256]{2,0,1:T(8,128)S(1)} %fusion.27), channel_id=1, replica_groups=mesh['rec'=16,'frame'=32] {'rec'}, use_global_device_ids=true, to_apply=%region_11.12 | all-reduce | flops 57345 | bytes 344072 | tf_op jit(solution)/shard_map/psum | solution.py:109
  788.0 0.6 dynamic-slice_convert_fusion
  (4 shorter events, 0.0 us)
Async XLA Ops:
  7.2 101.8 %copy-start = (bf16[1,1536,256]{2,1,0:T(8,128)(2,1)S(1)}, bf16[1,1536,256]{2,1,0:T(8,128)(2,1)}, u32[]{:S(2)}) copy-start(bf16[1,1536,256]{2,1,0:T(8,128)(2,1)} %param.5) | copy-start | bytes 2359300
  7.2 97.5 %all-gather.4.cloned.1.call-start = ((), (), s32[]{:S(2)}) async-start(), calls=%async_computation.1 | async-start | bytes 3899392 | tf_op jit(solution)/shard_map/all_gather | solution.py:51
  57.8 427.2 %all-gather.6.cloned.1.call-start = ((), (), s32[]{:S(2)}) async-start(), calls=%async_computation.3 | async-start | bytes 45416448 | tf_op jit(solution)/shard_map/all_gather | solution.py:72
  190.8 546.7 %reduce-scatter.3.cloned.1.call-start = ((), (), s32[]{:S(2)}) async-start(), calls=%async_computation.2 | async-start | bytes 1892352 | tf_op jit(solution)/shard_map/reduce_scatter | solution.py:87
  507.3 5.0 copy-start.1
  512.3 1.9 copy-start.3
  514.2 4.1 copy-start.2
  518.4 5.5 copy-start.4
Sparse Core Ops, SparseCore 0:
  57.9 46.7 all-gather.3
  191.0 293.9 all-gather.5
  516.5 220.9 reduce-scatter.2
